TPU v7x, 256 devices: a whole 4x4x8 slice. The times are simulated.
256 devices in a mesh: grp: 16 (over x, y), bal: 16 (over z, core).
Axes of the slice: x: 4, y: 4, z: 8, core: 2. Of those that a mesh axis runs over, the one named last changes fastest.
Arguments:
- node_grad: bfloat16 [2048, 49, 128], P(('grp', 'bal')), may hold values from -6 to 6
- coeffs_one: bfloat16 [65536, 29, 128], P(('grp', 'bal')), may hold values from -6 to 6
- coeffs_zero: bfloat16 [65536, 29, 128], P(('grp', 'bal')), may hold values from -6 to 6
- rotations: float32 [65536, 235], P(('grp', 'bal')), may hold values from -2 to 2
- weight_one: bfloat16 [29, 128, 128], replicated, may hold values from -0.5 to 0.5
- weight_two: bfloat16 [29, 128, 128], replicated, may hold values from -0.5 to 0.5
- sources: int32 [65536], P(('grp', 'bal')), may hold values from 0 to 127
- targets: int32 [65536], P(('grp', 'bal')), may hold values from 0 to 127, as said below
- edge_count: int32 [256], P(('grp', 'bal')), may hold values from 4 to 256, as said below
Outputs:
- node_out: float32 [2048, 49, 128], P(('grp', 'bal'))
- grad_one: float32 [29, 128, 128], replicated
- grad_two: float32 [29, 128, 128], replicated
Inputs may be any that keep to these rules, and one draw needn't show every extreme that they name: `edge_count`: some device has exactly 256 live slots in every draw. `targets`: the slots of the device at position p of bal target nodes p * 8 to (p + 1) * 8 - 1 of their graph.
All inputs are finite; a program needn't handle non-finite values.
Results may differ from a plain program's by a relative error of at most 0.0047.
Values may be sent and summed in bfloat16 or wider, within the bound.
A program may use at most 128 MiB of HBM per device.

v0:
```python
import jax
import jax.numpy as jnp
from jax import lax
from jax.sharding import PartitionSpec as P

BLOCK = 128


PAIRS = ((7, 13, 19), (19, 24, 29))
ORDER_BASE = (22, 12, 0, 6, 17)


def degree_starts():
    starts = []
    running = 0
    for degree in range(7):
        starts.append(running)
        running = running + (2 * min(degree, 2) + 1) * (2 * degree + 1)
    return starts


def rotation_block(rotation, degree, starts):
    kept = min(degree, 2)
    height = 2 * kept + 1
    width = 2 * degree + 1
    flat = rotation[:, starts[degree] : starts[degree] + height * width]
    return flat.reshape(flat.shape[0], height, width)


def rotate_in(rotation, node_rows):
    starts = degree_starts()
    placed = [None] * 29
    for degree in range(7):
        kept = min(degree, 2)
        block = rotation_block(rotation, degree, starts)
        turned = jnp.einsum(
            "emk,ekc->emc",
            block,
            node_rows[:, degree * degree : (degree + 1) * (degree + 1)],
            precision=lax.Precision.HIGHEST,
        )
        for order in range(-kept, kept + 1):
            placed[ORDER_BASE[order + 2] + degree] = turned[:, order + kept]
    return jnp.stack(placed, 1)


def rotate_out(rotation, edge_rows):
    starts = degree_starts()
    parts = []
    for degree in range(7):
        kept = min(degree, 2)
        block = rotation_block(rotation, degree, starts)
        picked = jnp.stack(
            [edge_rows[:, ORDER_BASE[order + 2] + degree] for order in range(-kept, kept + 1)], 1
        )
        parts.append(jnp.einsum("emk,emc->ekc", block, picked, precision=lax.Precision.HIGHEST))
    return jnp.concatenate(parts, 1)


def contract(first_operand, second_operand):
    return jnp.einsum(
        "erc,erd->rcd", first_operand, second_operand, preferred_element_type=jnp.float32
    )


def apply_weight(upstream_rows, weights):
    return jnp.einsum("erd,rcd->erc", upstream_rows, weights, preferred_element_type=jnp.float32)


def so2_grads(coeffs, upstream, weights):
    weight_parts = [contract(coeffs[:, :7], upstream[:, :7])]
    back_parts = [apply_weight(upstream[:, :7], weights[:7])]
    for plus_begin, minus_begin, minus_end in PAIRS:
        plus_in = coeffs[:, plus_begin:minus_begin]
        minus_in = coeffs[:, minus_begin:minus_end]
        plus_up = upstream[:, plus_begin:minus_begin]
        minus_up = upstream[:, minus_begin:minus_end]
        cosine_part = weights[plus_begin:minus_begin]
        sine_part = weights[minus_begin:minus_end]
        weight_parts.append(contract(plus_in, plus_up) + contract(minus_in, minus_up))
        weight_parts.append(contract(plus_in, minus_up) - contract(minus_in, plus_up))
        back_parts.append(apply_weight(plus_up, cosine_part) + apply_weight(minus_up, sine_part))
        back_parts.append(apply_weight(minus_up, cosine_part) - apply_weight(plus_up, sine_part))
    return (jnp.concatenate(weight_parts, 0), jnp.concatenate(back_parts, 1))


def on_device(
    node_grad,
    coeffs_one,
    coeffs_zero,
    rotations,
    weight_one,
    weight_two,
    sources,
    targets,
    edge_count,
):
    edges_dev = sources.shape[0]
    nodes_dev = node_grad.shape[0]
    group_nodes = nodes_dev * lax.axis_size("bal")
    valid_count = edge_count[0]
    used_blocks = (valid_count + BLOCK - 1) // BLOCK
    local_targets = targets - lax.axis_index("bal") * nodes_dev
    valid_slots = jnp.arange(edges_dev, dtype=jnp.int32) < valid_count

    def backward_layer(saved, upstream, weights):
        turned = rotate_in(rotations, upstream[local_targets].astype(jnp.float32))
        edge_up = jnp.where(valid_slots[:, None, None], turned, jnp.zeros((), jnp.float32)).astype(
            jnp.bfloat16
        )
        running = (
            jnp.zeros(weights.shape, jnp.float32),
            jnp.zeros((group_nodes, upstream.shape[1], upstream.shape[2]), jnp.float32),
        )

        def advance(position, totals):
            weight_total, node_tile = totals
            src_block = lax.dynamic_slice_in_dim(sources, position * BLOCK, BLOCK, 0)
            up_block = lax.dynamic_slice_in_dim(edge_up, position * BLOCK, BLOCK, 0)
            saved_block = lax.dynamic_slice_in_dim(saved, position * BLOCK, BLOCK, 0)
            rot_block = lax.dynamic_slice_in_dim(rotations, position * BLOCK, BLOCK, 0)
            weight_part, edge_back = so2_grads(saved_block, up_block, weights)
            node_back = rotate_out(rot_block, edge_back)
            return (weight_total + weight_part, node_tile.at[src_block].add(node_back))

        running = lax.fori_loop(0, used_blocks, advance, running)
        weight_total, node_tile = running
        partial_value = lax.psum_scatter(node_tile, "bal", scatter_dimension=0, tiled=True)
        return (weight_total, partial_value)

    grad_two, partial_two = backward_layer(coeffs_one, node_grad, weight_two)
    upstream_one = node_grad.astype(jnp.float32) + partial_two
    grad_one, partial_one = backward_layer(
        coeffs_zero, upstream_one.astype(jnp.bfloat16), weight_one
    )
    grad_one, grad_two = lax.psum((grad_one, grad_two), ("grp", "bal"))
    grad_scale = float(edges_dev * lax.axis_size("grp") * lax.axis_size("bal")) ** (-0.5)
    return (upstream_one + partial_one, grad_one * grad_scale, grad_two * grad_scale)


def solution(mesh):
    return jax.shard_map(
        on_device,
        mesh=mesh,
        in_specs=(
            P(("grp", "bal"), None, None),
            P(("grp", "bal"), None, None),
            P(("grp", "bal"), None, None),
            P(("grp", "bal"), None),
            P(),
            P(),
            P(("grp", "bal")),
            P(("grp", "bal")),
            P(("grp", "bal")),
        ),
        out_specs=(P(("grp", "bal"), None, None), P(), P()),
        check_vma=False,
    )
```

profile of v0, /device:TPU:1, one launch (start us, length us, event | category | flops | bytes accessed | tf_op | source)
XLA Modules:
  0.0 925.9 jit_solution(2884441591309246014)
XLA Ops:
  7.9 15.7 %gather_fusion = bf16[256,49,128]{2,0,1:T(8,128)(2,1)} fusion(bf16[8,49,128]{2,0,1:T(8,128)(2,1)} %param.13, s32[1024]{0:T(1024)S(1)} %pad_clamp_fusion), kind=kCustom, calls=%fused_computation | custom fusion | bytes 6423552 | tf_op jit(solution)/shard_map/gather | solution.py:107
  47.9 14.8 %stack.42 = bf16[256,29,128]{2,1,0:T(8,128)(2,1)} concatenate(f32[256,1,128]{2,1,0:T(1,128)} %bitcast.234, bf16[256,1,128]{2,1,0:T(2,128)(2,1)} %get-tuple-element.304, bf16[256,1,128]{2,1,0:T(2,128)(2,1)} %get-tuple-element.287, bf16[256,1,128]{2,1,0:T(2,128)(2,1)S(1)} %copy-done.35, bf16[256,1,128]{2,1,0:T(2,128)(2,1)S(1)} %copy-done.34, ...), dimensions={1} | concatenate | bytes 3866624 | tf_op jit(solution)/shard_map/stack | solution.py:44
  69.2 103.1 %while.24 = (s32[]{:T(128)}, f32[29,128,128]{2,1,0:T(8,128)}, f32[128,49,128]{2,1,0:T(8,128)}, s32[]{:T(128)}, bf16[256,29,128]{2,0,1:T(8,128)(2,1)}, /*index=5*...) while((s32[]{:T(128)}, f32[29,128,128]{2,1,0:T(8,128)}, ...), condition=%wide.region_2.3_spmd, body=%wide.region_0.2_spmd.sunk | while | flops 475939200 | bytes 87367344 | solution.py:126
  76.6 3.1 fusion.433
  81.6 4.0 fusion.432
  87.5 4.0 fusion.431
  93.4 3.1 fusion.430
  98.3 3.1 fusion.429
  108.2 28.3 %concatenate.14 = f32[128,49,128]{2,1,0:T(8,128)} concatenate(f32[128,1,128]{2,1,0:T(1,128)S(1)} %bitcast.232, f32[128,3,128]{2,1,0:T(4,128)} %fusion.426, f32[128,5,128]{2,1,0:T(8,128)} %fusion.429, f32[128,7,128]{2,1,0:T(8,128)} %fusion.430, f32[128,9,128]{2,1,0:T(8,128)} %fusion.431, f32[128,11,128]{2,1,0:T(8,128)} %fusion.432, f32[128,13,128]{2,1,0:T(8,128)S(1)} %fusion.433), dimensions={1} | concatenate | bytes 6422528 | tf_op jit(solution)/shard_map/while/body/concatenate | solution.py:57
  136.5 19.9 %scatter_fusion = f32[128,49,128]{2,1,0:T(8,128)} fusion(f32[128,49,128]{2,1,0:T(8,128)} %get-tuple-element.556, s32[128]{0:T(128)S(1)} %compare_select_fusion.5, f32[128,49,128]{2,1,0:T(8,128)} %concatenate.14), kind=kCustom, calls=%fused_computation.2.clone.1 | custom fusion | flops 802816 | bytes 9634304 | tf_op jit(solution)/shard_map/while/body/scatter-add | solution.py:124
  168.4 3.7 add.196
  172.3 165.1 %reduce-scatter.3.cloned.1.call-done = f32[8,49,128]{2,1,0:T(8,128)} async-done(((f32[128,49,128]{2,1,0:T(8,128)}), f32[8,49,128]{2,1,0:T(8,128)}) %reduce-scatter.3.cloned.1.call-update) | async-done | bytes 200720 | tf_op jit(solution)/shard_map/reduce_scatter | solution.py:128
  355.5 12.2 %stack.43 = bf16[256,29,128]{2,1,0:T(8,128)(2,1)} concatenate(f32[256,1,128]{2,1,0:T(1,128)S(1)} %bitcast.235, bf16[256,1,128]{2,1,0:T(2,128)(2,1)} %get-tuple-element.290, bf16[256,1,128]{2,1,0:T(2,128)(2,1)} %get-tuple-element.262, bf16[256,1,128]{2,1,0:T(2,128)(2,1)S(1)} %get-tuple-element.257, bf16[256,1,128]{2,1,0:T(2,128)(2,1)S(1)} %get-tuple-element.252, ...), dimensions={1} | concatenate | bytes 3866624 | tf_op jit(solution)/shard_map/stack | solution.py:44
  374.2 106.9 %while.25 = (s32[]{:T(128)}, f32[29,128,128]{2,1,0:T(8,128)}, f32[128,49,128]{2,1,0:T(8,128)}, s32[]{:T(128)}, bf16[256,29,128]{2,0,1:T(8,128)(2,1)}, /*index=5*...) while((s32[]{:T(128)}, f32[29,128,128]{2,1,0:T(8,128)}, ...), condition=%wide.region_6.7_spmd, body=%wide.region_4.6_spmd.sunk | while | flops 475939200 | bytes 87363232 | solution.py:126
  382.2 3.1 fusion.505
  388.5 4.1 fusion.504
  395.9 4.0 fusion.503
  401.8 3.1 fusion.502
  417.1 28.3 %concatenate.15 = f32[128,49,128]{2,1,0:T(8,128)} concatenate(f32[128,1,128]{2,1,0:T(1,128)} %bitcast.233, f32[128,3,128]{2,1,0:T(4,128)} %fusion.498, f32[128,5,128]{2,1,0:T(8,128)} %fusion.501, f32[128,7,128]{2,1,0:T(8,128)} %fusion.502, f32[128,9,128]{2,1,0:T(8,128)} %fusion.503, f32[128,11,128]{2,1,0:T(8,128)} %fusion.504, f32[128,13,128]{2,1,0:T(8,128)S(1)} %fusion.505), dimensions={1} | concatenate | bytes 6422528 | tf_op jit(solution)/shard_map/while/body/concatenate | solution.py:57
  445.5 19.9 %scatter_fusion.1 = f32[128,49,128]{2,1,0:T(8,128)} fusion(f32[128,49,128]{2,1,0:T(8,128)} %get-tuple-element.625, s32[128]{0:T(128)S(1)} %compare_select_fusion.6, f32[128,49,128]{2,1,0:T(8,128)} %concatenate.15), kind=kCustom, calls=%fused_computation.3.clone.1 | custom fusion | flops 802816 | bytes 9634304 | tf_op jit(solution)/shard_map/while/body/scatter-add | solution.py:124
  477.4 3.7 add.214
  481.9 373.4 %all-reduce.3.cloned.1.call-done = (f32[29,128,128]{2,1,0:T(8,128)}, f32[29,128,128]{2,1,0:T(8,128)}) async-done(((f32[29,128,128]{2,1,0:T(8,128)}, f32[29,128,128]{2,1,0:T(8,128)}), (f32[29,128,128]{2,1,0:T(8,128)}, f32[29,128,128]{2,1,0:T(8,128)})) %all-reduce.3.cloned.1.call-update) | async-done | bytes 3801104 | tf_op jit(solution)/shard_map/psum | solution.py:136
  855.3 3.1 broadcast_multiply_fusion
  859.9 57.4 %reduce-scatter.5.cloned.1.call-done = f32[8,49,128]{2,1,0:T(8,128)} async-done(((f32[128,49,128]{2,1,0:T(8,128)}), f32[8,49,128]{2,1,0:T(8,128)}) %reduce-scatter.5.cloned.1.call-update) | async-done | bytes 200720 | tf_op jit(solution)/shard_map/reduce_scatter | solution.py:128
  (262 shorter events, 133.0 us)
Async XLA Ops:
  7.2 330.3 %reduce-scatter.3.cloned.1.call-start = ((), (), s32[]{:S(2)}) async-start(), calls=%async_computation.2 | async-start | bytes 3899392 | tf_op jit(solution)/shard_map/reduce_scatter | solution.py:128
  24.7 7.7 copy-start.40
  27.2 9.6 %copy-start.21 = (f32[256,5,11]{2,1,0:T(8,128)}, f32[256,5,11]{2,1,0:T(8,128)S(1)}, u32[]{:S(2)}) copy-start(f32[256,5,11]{2,1,0:T(8,128)S(1)} %copy.96) | copy-start | bytes 168964
  27.2 6.8 slice-start
  31.3 5.5 slice-start.1
  34.0 28.7 %copy-start.42 = (pred[256]{0:T(512)(128)(4,1)}, pred[256]{0:T(512)(128)(4,1)S(1)}, u32[]{:S(2)}) copy-start(pred[256]{0:T(512)(128)(4,1)S(1)} %iota_compare_fusion) | copy-start | bytes 772
  40.9 3.1 slice-start.4
  40.9 3.1 copy-start.27
  65.6 3.5 copy-start.5
  108.2 28.3 %copy-start.44 = (s32[256]{0:T(256)S(1)}, s32[256]{0:T(256)}, u32[]{:S(2)}) copy-start(s32[256]{0:T(256)} %get-tuple-element.583) | copy-start | bytes 3076 | tf_op jit(solution)/shard_map/while
  164.1 3.2 copy-start.2
  168.4 3.7 copy-start.6
  172.2 165.2 %copy-start = (bf16[8,49,128]{2,0,1:T(8,128)(2,1)S(1)}, bf16[8,49,128]{2,0,1:T(8,128)(2,1)}, u32[]{:S(2)}) copy-start(bf16[8,49,128]{2,0,1:T(8,128)(2,1)} %param.13) | copy-start | bytes 301060
  172.3 683.0 %all-reduce.3.cloned.1.call-start = ((), (), s32[]{:S(2)}) async-start(), calls=%async_computation.4 | async-start | bytes 7602176 | tf_op jit(solution)/shard_map/psum | solution.py:136
  338.4 5.7 copy-start.22
  341.4 5.4 copy-start.19
  355.5 12.2 %copy-start.43 = (pred[256]{0:T(512)(128)(4,1)S(1)}, pred[256]{0:T(512)(128)(4,1)}, u32[]{:S(2)}) copy-start(pred[256]{0:T(512)(128)(4,1)} %copy-done.42) | copy-start | bytes 772
  370.6 3.5 copy-start.7
  370.6 3.5 copy-start.45
  473.1 3.2 copy-start.4
  477.4 3.7 copy-start.8
  481.1 436.1 %reduce-scatter.5.cloned.1.call-start = ((), (), s32[]{:S(2)}) async-start(), calls=%async_computation.3 | async-start | bytes 3899392 | tf_op jit(solution)/shard_map/reduce_scatter | solution.py:128
  855.3 3.1 copy-start.32
  858.4 58.8 %copy-start.33 = (f32[8,49,128]{2,1,0:T(8,128)S(1)}, f32[8,49,128]{2,1,0:T(8,128)}, u32[]{:S(2)}) copy-start(f32[8,49,128]{2,1,0:T(8,128)} %reduce-scatter.3.cloned.1.call-done) | copy-start | bytes 602116
  (31 other events, 49.4 us)
Sparse Core Ops, SparseCore 0:
  172.4 165.0 reduce-scatter.2
  481.2 373.9 all-reduce.2
  858.0 59.1 reduce-scatter.4
where the time goes:
time: 945 us; the launch traced here: 926 us
  waiting for transfers between devices  597 us (63%)
  local copies, waits for them, and re-layouts  162 us (17%)
  matrix products  86.6 us (9%)
  other arithmetic  64.5 us (7%)
  between operations  15.4 us (2%)
    psum x1, waiting for transfers between devices, on_device(): grad_one, grad_two = lax.psum((grad_one, grad_two), ('grp', 'bal'))  373 us
    reduce_scatter x2, waiting for transfers between devices, backward_layer(): lax.psum_scatter(node_tile, 'bal', scatter_dimension=0, tiled=True)  222 us
    concatenate x2, local copies, waits for them, and re-layouts, rotate_out(): return jnp.concatenate(parts, 1)  56.6 us
    dot_general x12, matrix products, rotate_out(): jnp.einsum('emk,emc->ekc', block, picked, precision=lax.Precision.HIGHEST)  40.1 us
    scatter-add x2, other arithmetic, advance(): return (weight_total + weight_part, node_tile.at[src_block].add(node_back))  39.7 us
    another operation x2, local copies, waits for them, and re-layouts, rotate_in(): return jnp.stack(placed, 1)  26.9 us
    dot_general x18, matrix products, contract(): jnp.einsum('erc,erd->rcd', first_operand, second_operand, preferred_eleme...  23.9 us
    reshape x36, local copies, waits for them, and re-layouts, rotation_block(): return flat.reshape(flat.shape[0], height, width)  20.7 us
  transfers between devices with their start and end apart: 3, of which 3 were waited for; matrix products, arithmetic and copies ran while one was open for 0% of the time, Pallas kernels for 0%

commit v1 on v0

v1 whole, which is shorter than its diff:
```python
import functools

import jax
import jax.numpy as jnp
from jax import lax
from jax.experimental import pallas as pl
from jax.experimental.pallas import tpu as pltpu
from jax.sharding import PartitionSpec as P

F32, BF16 = jnp.float32, jnp.bfloat16
MESH = pl.DeviceIdType.MESH

C = 128
COEF = 29
SPHERE = 49
WIGNER = 235
E = 256
T = 8
N_GRP = 16
N_Z = 8
ROWS = 400
SLOTS = 32
BASE = (22, 12, 0, 6, 17)
PAIRS = tuple((7 + i, 13 + i) for i in range(6)) + tuple((19 + i, 24 + i) for i in range(5))


def kept_of(degree):
    return min(degree, 2)


def height_of(degree):
    return 2 * kept_of(degree) + 1


def width_of(degree):
    return 2 * degree + 1


def depth_of(degree):
    return 128 if 16 * width_of(degree) <= 128 else 256


STARTS = []
AT_AT = []
_run = 0
_at = 0
for _l in range(7):
    STARTS.append(_run)
    AT_AT.append(_at)
    _run += height_of(_l) * width_of(_l)
    _at += height_of(_l) * depth_of(_l)
AT_ROWS = _at

PLACE = {r: r for r in range(7)}
for _i, (_p, _q) in enumerate(PAIRS):
    PLACE[_p] = 7 + 2 * _i
    PLACE[_q] = 8 + 2 * _i


def dot_nn(a, b):
    return lax.dot_general(a, b, (((1,), (0,)), ((), ())), preferred_element_type=F32)


def dot_nt(a, b):
    return lax.dot_general(a, b, (((1,), (1,)), ((), ())), preferred_element_type=F32)


def layer_kernel(
    rot_ref, src_ref, tgt_ref, count_ref, u_ref, x_ref, w_ref,
    p_ref, dw_ref,
    rpad, rt, at, gt, xf, sbuf, *dxs,
):
    rpad[:, 128:256] = jnp.zeros((E, 128), F32)
    rpad[:, 0:WIGNER] = rot_ref[...]
    rt[...] = rpad[...].T

    def unpack(e, carry):
        xf[pl.ds(pl.multiple_of(e * 32, 32), COEF), :] = x_ref[e].astype(F32)
        return carry

    lax.fori_loop(0, E, unpack, 0, unroll=8)

    lane = lax.broadcasted_iota(jnp.int32, (T, E), 1)
    spot = lax.broadcasted_iota(jnp.int32, (T, E), 0)
    hit = (spot == tgt_ref[...]) & (lane < count_ref[...])
    hot = jnp.where(hit, 1.0, 0.0).astype(F32)

    for l in range(7):
        width, height, depth = width_of(l), height_of(l), depth_of(l)
        rest = depth - 2 * T * width
        rows = u_ref[T * l * l : T * (l + 1) * (l + 1), :].astype(F32)
        twice = [rows, rows] + ([jnp.zeros((rest, C), F32)] if rest else [])
        ut = jnp.concatenate(twice, 0).T.astype(BF16)
        for m in range(height):
            first = STARTS[l] + m * width
            high, low = [], []
            for k in range(width):
                entry = hot * rt[first + k : first + k + 1, :]
                top = entry.astype(BF16).astype(F32)
                high.append(top)
                low.append(entry - top)
            pieces = high + low + ([jnp.zeros((rest, E), F32)] if rest else [])
            place = PLACE[BASE[m - kept_of(l) + 2] + l]
            turned = dot_nn(ut, jnp.concatenate(pieces, 0).astype(BF16))
            gt[place * C : (place + 1) * C, :] = turned.astype(BF16)

    def coeff(r):
        return xf[pl.ds(r, E, stride=32), :].astype(BF16)

    def put_dx(r, value):
        for l in range(7):
            for m in range(height_of(l)):
                if BASE[m - kept_of(l) + 2] + l == r:
                    dxs[l][:, m * E : (m + 1) * E] = value.astype(BF16)

    for r in range(7):
        g = gt[r * C : (r + 1) * C, :]
        dw_ref[r] = dot_nn(g, coeff(r)).T
        put_dx(r, dot_nn(w_ref[r], g))
    for i, (p, q) in enumerate(PAIRS):
        g = gt[(7 + 2 * i) * C : (9 + 2 * i) * C, :]
        both = dot_nn(g, jnp.concatenate([coeff(p), coeff(q)], 1))
        dw_ref[p] = (both[:C, :C] + both[C:, C:]).T
        dw_ref[q] = (both[C:, :C] - both[:C, C:]).T
        a, b = w_ref[p], w_ref[q]
        block = jnp.concatenate(
            [jnp.concatenate([a, b], 1), jnp.concatenate([-b, a], 1)], 0
        )
        back = dot_nn(block, g)
        put_dx(p, back[:C])
        put_dx(q, back[C:])
    for r in range(COEF, SLOTS):
        dw_ref[r] = jnp.zeros((C, C), F32)

    nodes = lax.broadcasted_iota(jnp.int32, (C, E), 0)
    at_source = jnp.where(nodes == src_ref[...], 1.0, 0.0).astype(F32)
    for l in range(7):
        width, height = width_of(l), height_of(l)
        for k in range(width):
            for m in range(height):
                j = STARTS[l] + m * width + k
                sbuf[l % 2, k * C : (k + 1) * C, m * E : (m + 1) * E] = (
                    at_source * rt[j : j + 1, :]
                ).astype(BF16)
        for k0 in range(0, width, 4):
            k1 = min(k0 + 4, width)
            got = dot_nt(sbuf[l % 2, k0 * C : k1 * C, : height * E], dxs[l][...])
            for k in range(k0, k1):
                row = l * l + k
                p_ref[:, row * T : (row + 1) * T, :] = got[
                    (k - k0) * C : (k - k0 + 1) * C
                ].reshape(C // T, T, C)
    p_ref[:, SPHERE * T : ROWS, :] = jnp.zeros((C // T, ROWS - SPHERE * T, C), F32)


def layer(rot, src, tgt, count, u, x, w):
    scratch = [
        pltpu.VMEM((E, 256), F32),
        pltpu.VMEM((256, E), F32),
        pltpu.VMEM((16, E), BF16),
        pltpu.VMEM((COEF * C, E), BF16),
        pltpu.VMEM((E * 32, C), F32),
        pltpu.VMEM((2, 13 * C, 5 * E), BF16),
    ] + [pltpu.VMEM((C, height_of(l) * E), BF16) for l in range(7)]
    return pl.pallas_call(
        layer_kernel,
        out_shape=(
            jax.ShapeDtypeStruct((C // T, ROWS, C), F32),
            jax.ShapeDtypeStruct((SLOTS, C, C), F32),
        ),
        in_specs=[pl.BlockSpec(memory_space=pltpu.VMEM)] * 7,
        out_specs=(pl.BlockSpec(memory_space=pltpu.VMEM),) * 2,
        scratch_shapes=scratch,
        compiler_params=pltpu.CompilerParams(vmem_limit_bytes=48 * 2**20),
        name="layer",
    )(rot, src, tgt, count, u, x, w)


def greet(q, z, c):
    barrier = pltpu.get_barrier_semaphore()
    b = 2 * z + c

    def signal(grp, bal):
        pl.semaphore_signal(
            barrier, inc=1, device_id={"grp": grp, "bal": bal}, device_id_type=MESH
        )

    signal(q, 2 * z + 1 - c)
    for i in range(1, N_Z):
        signal(q, lax.rem(z + i, N_Z) * 2 + c)
    for i in range(1, N_GRP):
        signal(lax.rem(q + i, N_GRP), b)
    pl.semaphore_wait(barrier, 1 + (N_Z - 1) + (N_GRP - 1))


def remote(src, dst, send, recv, grp, bal):
    return pltpu.make_async_remote_copy(
        src_ref=src, dst_ref=dst, send_sem=send, recv_sem=recv,
        device_id={"grp": grp, "bal": bal}, device_id_type=MESH,
    )


def comm_kernel(last, scale, *refs):
    if last:
        (p_ref, dw_ref, early_ref, part_ref, out_ref, *refs) = refs
    else:
        (p_ref, dw_ref, part_ref, shard_ref, *refs) = refs
    (cbuf, crecv, hop_s, hop_r, dcore, xy_s, xy_r, c_sem, hop_sem, d_sem, xy_sem, *refs) = refs
    if last:
        (zbuf, z_r, slot, z_sem, ag_sem, agxy_sem, fwd_sem) = refs
    q = lax.axis_index("grp")
    b = lax.axis_index("bal")
    z, c = lax.div(b, 2), lax.rem(b, 2)
    other = 2 * z + 1 - c
    greet(q, z, c)

    way = jnp.where(c == 0, N_Z - 1, 1)
    back = N_Z - way
    jobs = [("a", 4), ("b", 3), ("a", 3), ("b", 2), ("a", 2), ("b", 1), ("a", 1), ("own", 0)]

    def dest(chain, dist):
        step = way if chain == "a" else back
        return lax.rem(z + dist * step, N_Z) if dist else z

    sends = []
    for n, (chain, dist) in enumerate(jobs):
        d = dest("b" if chain == "a" else "a", dist)
        cbuf[n] = p_ref[2 * d + 1 - c].astype(BF16)
        copy = remote(cbuf.at[n], crecv.at[n], c_sem.at[0, n], c_sem.at[1, n], q, other)
        copy.start()
        sends.append(copy)
    dcopy = remote(dw_ref.at[pl.ds((1 - c) * 16, 16)], dcore, d_sem.at[0], d_sem.at[1], q, other)
    dcopy.start()

    hops = {}
    order = {("a", 4): 0, ("a", 3): 1, ("a", 2): 2, ("a", 1): 3, ("b", 3): 4, ("b", 2): 5, ("b", 1): 6}

    def chain_step(n):
        chain, dist = jobs[n]
        d = dest(chain, dist)
        sends[n].wait_recv()
        value = p_ref[2 * d + c] + crecv[n].astype(F32)
        before = (chain, dist + 1)
        if chain != "own" and before in order:
            hops[before].wait_recv()
            value += hop_r[order[before]].astype(F32)
        if chain == "own":
            for before in (("a", 1), ("b", 1)):
                hops[before].wait_recv()
                value += hop_r[order[before]].astype(F32)
            part_ref[...] = value
            return
        h = order[(chain, dist)]
        hop_s[h] = value.astype(BF16)
        target = lax.rem(z + (way if chain == "a" else back), N_Z)
        copy = remote(hop_s.at[h], hop_r.at[h], hop_sem.at[0, h], hop_sem.at[1, h], q, 2 * target + c)
        copy.start()
        hops[(chain, dist)] = copy

    chain_step(0)
    chain_step(1)

    dcopy.wait_recv()
    xys = []
    for i in range(1, N_GRP):
        to = lax.rem(q + i, N_GRP)
        xy_s[i - 1] = (dw_ref[c * 16 + to] + dcore[to]).astype(BF16)
        copy = remote(xy_s.at[i - 1], xy_r.at[i - 1], xy_sem.at[0, i - 1], xy_sem.at[1, i - 1], to, b)
        copy.start()
        xys.append(copy)

    chain_step(2)
    chain_step(3)

    def plane_sum():
        total = dw_ref[c * 16 + q] + dcore[q]
        for i in range(1, N_GRP):
            xys[i - 1].wait_recv()
            total += xy_r[i - 1].astype(F32)
        return total

    if not last:
        for n in range(4, 8):
            chain_step(n)
        shard_ref[...] = plane_sum()
        pending = []
    else:
        zbuf[0] = plane_sum()
        zbuf[1] = early_ref[...]
        zs = []
        for i in range(1, N_Z):
            to = lax.rem(z + i, N_Z)
            rows = pl.ds(pl.multiple_of(to * 16, 16), 16)
            copy = remote(zbuf.at[:, rows, :], z_r.at[i - 1], z_sem.at[0, i - 1], z_sem.at[1, i - 1], q, 2 * to + c)
            copy.start()
            zs.append(copy)
        chain_step(4)
        chain_step(5)
        mine = pl.ds(pl.multiple_of(z * 16, 16), 16)
        total = zbuf[:, mine, :]
        for i in range(1, N_Z):
            zs[i - 1].wait_recv()
            total += z_r[i - 1]
        slot[:, mine, :] = (total * scale).astype(BF16)
        ags = []
        for i in range(1, N_Z):
            to = lax.rem(z + i, N_Z)
            copy = remote(slot.at[:, mine, :], slot.at[:, mine, :], ag_sem.at[0, i - 1], ag_sem.at[1, i - 1], q, 2 * to + c)
            copy.start()
            ags.append(copy)
        chain_step(6)
        for i in range(1, N_Z):
            rows = pl.ds(pl.multiple_of(lax.rem(z + N_Z - i, N_Z) * 16, 16), 16)
            remote(slot.at[:, rows, :], slot.at[:, rows, :], ag_sem.at[0, i - 1], ag_sem.at[1, i - 1], q, b).wait_recv()
        for i in range(1, N_Z):
            ags[i - 1].wait_send()
        agxys = []
        for i in range(1, N_GRP):
            to = lax.rem(q + i, N_GRP)
            copy = remote(slot, out_ref.at[:, c * 16 + q], agxy_sem.at[0, i - 1], agxy_sem.at[1, i - 1], to, b)
            copy.start()
            agxys.append(copy)
        out_ref[:, c * 16 + q] = slot[...]
        fwds = [remote(slot, out_ref.at[:, c * 16 + q], fwd_sem.at[0, 0], fwd_sem.at[1, 0], q, other)]
        fwds[0].start()
        chain_step(7)
        for i in range(1, N_GRP):
            came = c * 16 + lax.rem(q + N_GRP - i, N_GRP)
            remote(slot, out_ref.at[:, came], agxy_sem.at[0, i - 1], agxy_sem.at[1, i - 1], q, b).wait_recv()
            copy = remote(out_ref.at[:, came], out_ref.at[:, came], fwd_sem.at[0, i], fwd_sem.at[1, i], q, other)
            copy.start()
            fwds.append(copy)
        for i in range(N_GRP):
            came = (1 - c) * 16 + lax.rem(q + N_GRP - i, N_GRP)
            remote(slot, out_ref.at[:, came], fwd_sem.at[0, i], fwd_sem.at[1, i], q, b).wait_recv()
        pending = zs + agxys + fwds
    for copy in sends + [dcopy] + list(hops.values()) + xys + pending:
        copy.wait_send()


def comm(last, scale, *args):
    dma = pltpu.SemaphoreType.DMA
    scratch = [
        pltpu.VMEM((N_Z, ROWS, C), BF16),
        pltpu.VMEM((N_Z, ROWS, C), BF16),
        pltpu.VMEM((N_Z - 1, ROWS, C), BF16),
        pltpu.VMEM((N_Z - 1, ROWS, C), BF16),
        pltpu.VMEM((16, C, C), F32),
        pltpu.VMEM((N_GRP - 1, C, C), BF16),
        pltpu.VMEM((N_GRP - 1, C, C), BF16),
        dma((2, N_Z)),
        dma((2, N_Z - 1)),
        dma((2,)),
        dma((2, N_GRP - 1)),
    ]
    outs = [jax.ShapeDtypeStruct((ROWS, C), F32)]
    if last:
        scratch += [
            pltpu.VMEM((2, C, C), F32),
            pltpu.VMEM((N_Z - 1, 2, 16, C), F32),
            pltpu.VMEM((2, C, C), BF16),
            dma((2, N_Z - 1)),
            dma((2, N_Z - 1)),
            dma((2, N_GRP - 1)),
            dma((2, N_GRP)),
        ]
        outs.append(jax.ShapeDtypeStruct((2, SLOTS, C, C), BF16))
    else:
        outs.append(jax.ShapeDtypeStruct((C, C), F32))
    return pl.pallas_call(
        functools.partial(comm_kernel, last, scale),
        out_shape=tuple(outs),
        in_specs=[pl.BlockSpec(memory_space=pltpu.VMEM)] * len(args),
        out_specs=(pl.BlockSpec(memory_space=pltpu.VMEM),) * 2,
        scratch_shapes=scratch,
        compiler_params=pltpu.CompilerParams(
            collective_id=1 if last else 0, has_side_effects=True, vmem_limit_bytes=48 * 2**20
        ),
        name="comm_last" if last else "comm_first",
    )(*args)


def on_device(
    node_grad, coeffs_one, coeffs_zero, rotations, weight_one, weight_two, sources, targets, edge_count
):
    scale = float(sources.shape[0] * lax.axis_size("grp") * lax.axis_size("bal")) ** (-0.5)
    src = sources.reshape(1, E)
    tgt = (targets - lax.axis_index("bal") * T).reshape(1, E)
    count = edge_count.reshape(1, 1)
    top = jnp.transpose(node_grad, (1, 0, 2)).reshape(SPHERE * T, C).astype(F32)
    top = jnp.pad(top, ((0, ROWS - SPHERE * T), (0, 0)))

    sums_two, dw_two = layer(rotations, src, tgt, count, top, coeffs_one, weight_two)
    part_two, shard_two = comm(False, scale, sums_two, dw_two)
    up_one = top + part_two
    sums_one, dw_one = layer(
        rotations, src, tgt, count, up_one.astype(BF16), coeffs_zero, weight_one
    )
    part_one, grads = comm(True, scale, sums_one, dw_one, shard_two)
    node_out = (up_one + part_one)[: SPHERE * T].reshape(SPHERE, T, C).transpose(1, 0, 2)
    return node_out, grads[0, :COEF].astype(F32), grads[1, :COEF].astype(F32)


def solution(mesh):
    both = P(("grp", "bal"))
    return jax.shard_map(
        on_device,
        mesh=mesh,
        in_specs=(
            P(("grp", "bal"), None, None),
            P(("grp", "bal"), None, None),
            P(("grp", "bal"), None, None),
            P(("grp", "bal"), None),
            P(),
            P(),
            both,
            both,
            both,
        ),
        out_specs=(P(("grp", "bal"), None, None), P(), P()),
        check_vma=False,
    )
```

time: 945 us -> 106 us (0.11); the launches traced: 926 us -> 106 us
  waiting for transfers between devices: 597 us -> 0 us
  local copies, waits for them, and re-layouts: 162 us -> 7.05 us
  Pallas kernels: 0 us -> 92.6 us
  matrix products: 86.6 us -> 0 us
  other arithmetic: 64.5 us -> 4.75 us
  between operations: 15.4 us -> 1.39 us
    psum x1 -> x0, waiting for transfers between devices: 373 us -> none  [on_device(): grad_one, grad_two = lax.psum((grad_one, grad_two), ('grp', 'bal'))]
    reduce_scatter x2 -> x0, waiting for transfers between devices: 222 us -> none  [backward_layer(): lax.psum_scatter(node_tile, 'bal', scatter_dimension=0, tiled=True)]
    pallas_call x0 -> x4, Pallas kernels: none -> 92.6 us  [the longest x2 72.7 us: comm(): pl.pallas_call(functools.partial(comm_kernel, last, scale), out_shape=tup...]
    dot_general x60 -> x0, matrix products: 86.6 us -> none  [the longest x12 40.1 us: rotate_out(): jnp.einsum('emk,emc->ekc', block, picked, precision=lax.Precision.HIGHEST)]
    concatenate x2 -> x0, local copies, waits for them, and re-layouts: 56.6 us -> none  [rotate_out(): return jnp.concatenate(parts, 1)]
    scatter-add x2 -> x0, other arithmetic: 39.7 us -> none  [advance(): return (weight_total + weight_part, node_tile.at[src_block].add(node_back))]
    another operation x9 -> x0, local copies, waits for them, and re-layouts: 34.7 us -> none  [the longest x2 26.9 us: rotate_in(): return jnp.stack(placed, 1)]
    reshape x37 -> x0, local copies, waits for them, and re-layouts: 21.4 us -> none  [the longest x36 20.7 us: rotation_block(): return flat.reshape(flat.shape[0], height, width)]
  transfers between devices with their start and end apart: 3 -> 0, of which waited for: 3 -> 0; matrix products, arithmetic and copies ran while one was open for 0% -> 0% of each run, Pallas kernels for 0% -> 0%
where the time goes in v1:
time: 106 us
  Pallas kernels  92.6 us (87%)
  local copies, waits for them, and re-layouts  7.05 us (7%)
  other arithmetic  4.75 us (4%)
  between operations  1.39 us (1%)
    pallas_call x2, Pallas kernels, comm(): pl.pallas_call(functools.partial(comm_kernel, last, scale), out_shape=tup...  72.7 us
    pallas_call x2, Pallas kernels, layer(): pl.pallas_call(layer_kernel, out_shape=(jax.ShapeDtypeStruct((C // T, ROW...  19.9 us
    unnamed x15, local copies, waits for them, and re-layouts  7.05 us
    convert_element_type x1, other arithmetic, on_device(): return (node_out, grads[0, :COEF].astype(F32), grads[1, :COEF].astype(F32))  2.34 us

profile of v1, /device:TPU:1, one launch (start us, length us, event | category | flops | bytes accessed | tf_op | source)
XLA Modules:
  0.0 105.8 jit_solution(17602832725660568350)
XLA Ops:
  0.6 1.1 %copy.12.rot_ref = f32[256,235]{1,0:T(8,128)S(1)} copy(f32[256,235]{0,1:T(8,128)} %param.12) | data formatting | bytes 481280 | tf_op args[3]
  1.7 0.0 copy-start.1
  1.7 0.0 copy-start.3
  1.7 1.0 pad_convert_fusion.u_ref
  2.7 0.7 broadcast_subtract_fusion
  4.1 2.8 %copy.13.x_ref = bf16[256,29,128]{2,1,0:T(8,128)(2,1)S(1)} copy(bf16[256,29,128]{2,0,1:T(8,128)(2,1)} %param.10) | data formatting | bytes 3801088 | tf_op args[1]
  6.8 0.0 copy-done.1
  6.9 0.0 copy-done.3
  6.9 9.8 %layer.2 = (f32[16,400,128]{2,1,0:T(8,128)}, f32[32,128,128]{2,1,0:T(8,128)S(1)}) custom-call(f32[256,235]{1,0:T(8,128)S(1)} %copy.12.rot_ref, s32[1,256]{1,0:T(1,128)S(1)} %bitcast.20, s32[1,256]{1,0:T(1,128)S(1)} %bitcast.18, s32[1,1]{1,0:T(1,128)} %bitcast.16.count_ref, f32[400,128]{1,0:T(8,128)S(1)} %pad_convert_fusion.u_ref, ...), custom_call_target="tpu_custom_call" | custom-call | tf_op jit(solution)/shard_map/layer/pallas_call | solution.py:165
  16.7 0.0 copy-start
  16.7 1.9 %copy-done = f32[16,400,128]{2,1,0:T(8,128)S(1)} copy-done((f32[16,400,128]{2,1,0:T(8,128)S(1)}, f32[16,400,128]{2,1,0:T(8,128)}, u32[]{:S(2)}) %copy-start) | copy-done | bytes 3276824
  18.6 0.0 copy-start.5
  18.6 0.0 copy-start.4
  18.6 27.5 %comm_first.1 = (f32[400,128]{1,0:T(8,128)S(1)}, f32[128,128]{1,0:T(8,128)S(1)}) custom-call(f32[16,400,128]{2,1,0:T(8,128)S(1)} %copy-done, f32[32,128,128]{2,1,0:T(8,128)S(1)} %get-tuple-element.12.refs_1_), custom_call_target="tpu_custom_call" | custom-call | tf_op jit(solution)/shard_map/comm_first/pallas_call | solution.py:370
  46.1 0.0 copy-done.5
  46.1 0.0 copy-start.2
  46.1 0.0 copy-done.4
  46.2 1.3 %copy.15.x_ref = bf16[256,29,128]{2,1,0:T(8,128)(2,1)S(1)} copy(bf16[256,29,128]{2,0,1:T(8,128)(2,1)S(1)} %copy-done.4) | data formatting | bytes 3801088 | tf_op args[2]
  47.4 0.0 copy-done.2
  47.4 10.1 %layer.3 = (f32[16,400,128]{2,1,0:T(8,128)}, f32[32,128,128]{2,1,0:T(8,128)S(1)}) custom-call(f32[256,235]{1,0:T(8,128)S(1)} %copy.12.rot_ref, s32[1,256]{1,0:T(1,128)S(1)} %bitcast.21, s32[1,256]{1,0:T(1,128)S(1)} %bitcast.19, s32[1,1]{1,0:T(1,128)} %bitcast.17.count_ref, bf16[400,128]{1,0:T(8,128)(2,1)S(1)} %get-tuple-element.19.u_ref, ...), custom_call_target="tpu_custom_call" | custom-call | tf_op jit(solution)/shard_map/layer/pallas_call | solution.py:165
  57.5 45.3 %comm_last.1 = (f32[400,128]{1,0:T(8,128)S(1)}, bf16[2,32,128,128]{3,2,1,0:T(8,128)(2,1)S(1)}) custom-call(f32[16,400,128]{2,1,0:T(8,128)} %get-tuple-element.14.refs_0_, f32[32,128,128]{2,1,0:T(8,128)S(1)} %get-tuple-element.15.refs_1_, f32[128,128]{1,0:T(8,128)S(1)} %get-tuple-element.16.refs_2_), custom_call_target="tpu_custom_call" | custom-call | tf_op jit(solution)/shard_map/comm_last/pallas_call | solution.py:370
  102.8 2.3 %bitcast_convert_fusion = (f32[29,128,128]{2,1,0:T(8,128)}, f32[29,128,128]{2,1,0:T(8,128)}) fusion(bf16[2,32,128,128]{3,2,1,0:T(8,128)(2,1)S(1)} %get-tuple-element.18), kind=kLoop, calls=%fused_computation | loop fusion | flops 950272 | bytes 5701632 | tf_op jit(solution)/shard_map/convert_element_type | solution.py:401
  105.1 0.7 fusion
  (1 shorter events, 0.0 us)
Async XLA Ops:
  1.7 5.1 %copy-start.1 = (bf16[29,128,128]{2,1,0:T(8,128)(2,1)S(1)}, bf16[29,128,128]{2,1,0:T(8,128)(2,1)}, u32[]{:S(2)}) copy-start(bf16[29,128,128]{2,1,0:T(8,128)(2,1)} %w_ref.2) | copy-start | bytes 2850820
  1.7 5.1 %copy-start.3 = (s32[256]{0:T(256)S(1)}, s32[256]{0:T(256)}, u32[]{:S(2)}) copy-start(s32[256]{0:T(256)} %param.15) | copy-start | bytes 3076
  16.7 1.9 %copy-start = (f32[16,400,128]{2,1,0:T(8,128)S(1)}, f32[16,400,128]{2,1,0:T(8,128)}, u32[]{:S(2)}) copy-start(f32[16,400,128]{2,1,0:T(8,128)} %get-tuple-element.11.refs_0_) | copy-start | bytes 9830404
  18.6 27.5 %copy-start.5 = (bf16[8,49,128]{2,0,1:T(8,128)(2,1)S(1)}, bf16[8,49,128]{2,0,1:T(8,128)(2,1)}, u32[]{:S(2)}) copy-start(bf16[8,49,128]{2,0,1:T(8,128)(2,1)} %param.9) | copy-start | bytes 301060
  18.6 27.5 %copy-start.4 = (bf16[256,29,128]{2,0,1:T(8,128)(2,1)S(1)}, bf16[256,29,128]{2,0,1:T(8,128)(2,1)}, u32[]{:S(2)}) copy-start(bf16[256,29,128]{2,0,1:T(8,128)(2,1)} %param.11) | copy-start | bytes 5701636
  46.1 1.3 %copy-start.2 = (bf16[29,128,128]{2,1,0:T(8,128)(2,1)S(1)}, bf16[29,128,128]{2,1,0:T(8,128)(2,1)}, u32[]{:S(2)}) copy-start(bf16[29,128,128]{2,1,0:T(8,128)(2,1)} %w_ref.3) | copy-start | bytes 2850820

commit v2 on v0

v2 whole, which is shorter than its diff:
```python
import functools

import jax
import jax.numpy as jnp
from jax import lax
from jax.experimental import pallas as pl
from jax.experimental.pallas import tpu as pltpu
from jax.sharding import PartitionSpec as P

F32, BF16 = jnp.float32, jnp.bfloat16
MESH = pl.DeviceIdType.MESH

C = 128
COEF = 29
SPHERE = 49
WIGNER = 235
E = 256
T = 8
N_GRP = 16
N_Z = 8
ROWS = 400
SLOTS = 32
BASE = (22, 12, 0, 6, 17)
PAIRS = tuple((7 + i, 13 + i) for i in range(6)) + tuple((19 + i, 24 + i) for i in range(5))


def kept_of(degree):
    return min(degree, 2)


def height_of(degree):
    return 2 * kept_of(degree) + 1


def width_of(degree):
    return 2 * degree + 1


def depth_of(degree):
    return 128 if 16 * width_of(degree) <= 128 else 256


STARTS = []
AT_AT = []
_run = 0
_at = 0
for _l in range(7):
    STARTS.append(_run)
    AT_AT.append(_at)
    _run += height_of(_l) * width_of(_l)
    _at += height_of(_l) * depth_of(_l)
AT_ROWS = _at

PLACE = {r: r for r in range(7)}
for _i, (_p, _q) in enumerate(PAIRS):
    PLACE[_p] = 7 + 2 * _i
    PLACE[_q] = 8 + 2 * _i


def dot_nn(a, b):
    return lax.dot_general(a, b, (((1,), (0,)), ((), ())), preferred_element_type=F32)


def dot_nt(a, b):
    return lax.dot_general(a, b, (((1,), (1,)), ((), ())), preferred_element_type=F32)


SINGLES = tuple(range(7))
ITEMS = SINGLES + PAIRS
CHUNKS = (((6,), 288, 112), ((4, 5), 128, 160), ((0, 1, 2, 3), 0, 128))
LIVE = SPHERE * T
OFFSETS = (
    (1, 0), (0, 1), (3, 0), (0, 3), (1, 1), (3, 3), (1, 3), (3, 1),
    (2, 0), (0, 2), (2, 1), (1, 2), (2, 3), (3, 2), (2, 2),
)
HOP = {("a", 4): 0, ("a", 3): 1, ("a", 2): 2, ("a", 1): 3, ("b", 3): 4, ("b", 2): 5, ("b", 1): 6}
STEPS = (
    (("a", 4), ("b", 3)), (("a", 3), ("b", 2)), (("a", 2), ("b", 1)), (("a", 1),), (("own", 0),),
)


def remote(src, dst, send, recv, grp, bal):
    return pltpu.make_async_remote_copy(
        src_ref=src, dst_ref=dst, send_sem=send, recv_sem=recv,
        device_id={"grp": grp, "bal": bal}, device_id_type=MESH,
    )


def kernel(
    scale,
    rot_ref, src_ref, tgt_ref, count_ref, top_ref, x_two, x_one, w_two, w_one,
    node_ref, out_ref,
    xs, ws, up, at, gt, sbuf, p, cbuf, crecv, hop_s, hop_r,
    dw, dcore, xy_s, xy_r, zbuf, z_r, slot,
    in_sem, c_sem, hop_sem, d_sem, xy_sem, z_sem, ag_sem, agxy_sem, fwd_sem,
    *dxs,
):
    q = lax.axis_index("grp")
    b = lax.axis_index("bal")
    z, c = lax.div(b, 2), lax.rem(b, 2)
    px, py = lax.div(q, 4), lax.rem(q, 4)
    other = 2 * z + 1 - c

    def plane(dx, dy):
        return lax.rem(px + dx, 4) * 4 + lax.rem(py + dy, 4)

    ahead = [plane(dx, dy) for dx, dy in OFFSETS]
    behind = [plane(4 - dx, 4 - dy) for dx, dy in OFFSETS]

    barrier = pltpu.get_barrier_semaphore()

    def signal(grp, bal):
        pl.semaphore_signal(
            barrier, inc=1, device_id={"grp": grp, "bal": bal}, device_id_type=MESH
        )

    signal(q, other)
    for i in range(1, N_Z):
        signal(q, lax.rem(z + i, N_Z) * 2 + c)
    for to in ahead:
        signal(to, b)

    loads = {}
    for n, (name, src, dst) in enumerate((
        ("w0", w_two, ws.at[0]), ("x0", x_two, xs.at[0]), ("w1", w_one, ws.at[1]), ("x1", x_one, xs.at[1]),
    )):
        loads[name] = pltpu.make_async_copy(src, dst, in_sem.at[n])
        loads[name].start()

    up[0:LIVE] = top_ref[...].astype(F32)
    up[LIVE:ROWS] = jnp.zeros((ROWS - LIVE, C), F32)
    p[:, :, LIVE:ROWS] = jnp.zeros((N_Z, 2, ROWS - LIVE, C), F32)

    def front(layer):
        if layer == 0:
            lane = lax.broadcasted_iota(jnp.int32, (T, E), 1)
            spot = lax.broadcasted_iota(jnp.int32, (T, E), 0)
            hit = (spot == tgt_ref[...] - b * T) & (lane < count_ref[...])
            hot = jnp.where(hit, 1.0, 0.0).astype(F32)
        for l in range(7):
            width, height, depth = width_of(l), height_of(l), depth_of(l)
            rest = depth - 2 * T * width
            rows = up[T * l * l : T * (l + 1) * (l + 1), :]
            twice = [rows, rows] + ([jnp.zeros((rest, C), F32)] if rest else [])
            ut = jnp.concatenate(twice, 0).T.astype(BF16)
            for m in range(height):
                first = AT_AT[l] + m * depth
                if layer == 0:
                    high, low = [], []
                    for k in range(width):
                        j = STARTS[l] + m * width + k
                        entry = hot * rot_ref[j : j + 1, :]
                        top = entry.astype(BF16).astype(F32)
                        high.append(top)
                        low.append(entry - top)
                    pieces = high + low + ([jnp.zeros((rest, E), F32)] if rest else [])
                    at[first : first + depth, :] = jnp.concatenate(pieces, 0).astype(BF16)
                place = PLACE[BASE[m - kept_of(l) + 2] + l]
                turned = dot_nn(ut, at[first : first + depth, :])
                gt[place * C : (place + 1) * C, :] = turned.astype(BF16)

    def weight_grads(layer, items):
        for item in items:
            if isinstance(item, int):
                g = gt[item * C : (item + 1) * C, :]
                dw[layer, item] = dot_nn(g, xs[layer, item]).T
                continue
            r, s = item
            g = gt[PLACE[r] * C : (PLACE[r] + 2) * C, :]
            both = dot_nn(g, jnp.concatenate([xs[layer, r], xs[layer, s]], 1))
            dw[layer, r] = (both[:C, :C] + both[C:, C:]).T
            dw[layer, s] = (both[C:, :C] - both[:C, C:]).T

    for layer in range(2):
        for r in range(COEF, SLOTS):
            dw[layer, r] = jnp.zeros((C, C), F32)

    def put_dx(r, value):
        high = value.astype(BF16)
        low = (value - high.astype(F32)).astype(BF16)
        for l in range(7):
            for m in range(height_of(l)):
                if BASE[m - kept_of(l) + 2] + l == r:
                    dxs[l][0:C, m * E : (m + 1) * E] = high
                    dxs[l][C : 2 * C, m * E : (m + 1) * E] = low

    def edge_back(layer):
        for item in ITEMS:
            if isinstance(item, int):
                put_dx(item, dot_nn(ws[layer, item], gt[item * C : (item + 1) * C, :]))
                continue
            r, s = item
            g = gt[PLACE[r] * C : (PLACE[r] + 2) * C, :]
            cosine, sine = ws[layer, r], ws[layer, s]
            block = jnp.concatenate(
                [jnp.concatenate([cosine, sine], 1), jnp.concatenate([-sine, cosine], 1)], 0
            )
            back = dot_nn(block, g)
            put_dx(r, back[:C])
            put_dx(s, back[C:])

    def outward(layer, chunk):
        degrees, begin, count = CHUNKS[chunk]
        for l in degrees:
            width, height = width_of(l), height_of(l)
            if layer == 0:
                nodes = lax.broadcasted_iota(jnp.int32, (C, E), 0)
                at_source = jnp.where(nodes == src_ref[...], 1.0, 0.0).astype(F32)
                for k in range(width):
                    for m in range(height):
                        j = STARTS[l] + m * width + k
                        sbuf[l][k * C : (k + 1) * C, m * E : (m + 1) * E] = (
                            at_source * rot_ref[j : j + 1, :]
                        ).astype(BF16)
            for k0 in range(0, width, 4):
                k1 = min(k0 + 4, width)
                got = dot_nt(sbuf[l][k0 * C : k1 * C, :], dxs[l][...])
                got = got[:, :C] + got[:, C:]
                for k in range(k0, k1):
                    row = l * l + k
                    p[:, :, row * T : (row + 1) * T, :] = got[
                        (k - k0) * C : (k - k0 + 1) * C
                    ].reshape(N_Z, 2, T, C)

    way = jnp.where(c == 0, N_Z - 1, 1)
    step_of = {"a": way, "b": N_Z - way, "own": way}
    started = []

    def start(copy):
        copy.start()
        started.append(copy)
        return copy

    def rows_of(chunk):
        _, begin, count = CHUNKS[chunk]
        return slice(begin, begin + count)

    cores, hops, cross, planes, lines, spreads, wides = {}, {}, {}, {}, {}, {}, {}

    def core_send(layer, chunk):
        rows = rows_of(chunk)
        cbuf[layer, :, rows] = p[:, 1 - c, rows].astype(BF16)
        view = (layer, slice(None), pl.ds(rows.start, rows.stop - rows.start))
        cores[layer, chunk] = start(remote(
            cbuf.at[view], crecv.at[view], c_sem.at[0, layer, chunk], c_sem.at[1, layer, chunk], q, other
        ))

    def chain(layer, chunk, step):
        rows = rows_of(chunk)
        if step == 0:
            cores[layer, chunk].wait_recv()
        for name, dist in STEPS[step]:
            d = lax.rem(z + dist * step_of[name], N_Z)
            value = p[d, c, rows] + crecv[layer, d, rows].astype(F32)
            before = (("a", 1), ("b", 1)) if name == "own" else ((name, dist + 1),)
            for key in before:
                if key in HOP:
                    hops[layer, chunk, key].wait_recv()
                    value += hop_r[layer, HOP[key], rows].astype(F32)
            if name == "own":
                live = min(rows.stop, LIVE) - rows.start
                kept = slice(rows.start, rows.start + live)
                if layer == 0:
                    up[kept] = up[kept] + value[:live]
                else:
                    node_ref[kept] = up[kept] + value[:live]
                continue
            h = HOP[name, dist]
            hop_s[layer, h, rows] = value.astype(BF16)
            view = (layer, h, pl.ds(rows.start, rows.stop - rows.start))
            to = 2 * lax.rem(z + step_of[name], N_Z) + c
            hops[layer, chunk, (name, dist)] = start(remote(
                hop_s.at[view], hop_r.at[view], hop_sem.at[0, layer, chunk, h], hop_sem.at[1, layer, chunk, h], q, to
            ))

    def d_send(layer):
        half = pl.ds((1 - c) * 16, 16)
        cross[layer] = start(remote(
            dw.at[layer, half], dcore.at[layer], d_sem.at[0, layer], d_sem.at[1, layer], q, other
        ))

    def xy_send(layer):
        cross[layer].wait_recv()
        for i, to in enumerate(ahead):
            xy_s[layer, i] = (dw[layer, c * 16 + to] + dcore[layer, to]).astype(BF16)
            planes[layer, i] = start(remote(
                xy_s.at[layer, i], xy_r.at[layer, i], xy_sem.at[0, layer, i], xy_sem.at[1, layer, i], to, b
            ))

    def z_send(layer):
        total = dw[layer, c * 16 + q] + dcore[layer, q]
        for i in range(N_GRP - 1):
            planes[layer, i].wait_recv()
            total += xy_r[layer, i].astype(F32)
        zbuf[layer] = total
        for i in range(1, N_Z):
            to = lax.rem(z + i, N_Z)
            rows = pl.ds(pl.multiple_of(to * 16, 16), 16)
            lines[layer, i] = start(remote(
                zbuf.at[layer, rows], z_r.at[layer, i - 1], z_sem.at[0, layer, i - 1], z_sem.at[1, layer, i - 1],
                q, 2 * to + c,
            ))

    mine = pl.ds(pl.multiple_of(z * 16, 16), 16)

    def z_sum(layer):
        total = zbuf[layer, mine, :]
        for i in range(1, N_Z):
            lines[layer, i].wait_recv()
            total += z_r[layer, i - 1]
        slot[layer, mine, :] = (total * scale).astype(BF16)
        for i in range(1, N_Z):
            to = lax.rem(z + i, N_Z)
            spreads[layer, i] = start(remote(
                slot.at[layer, mine], slot.at[layer, mine], ag_sem.at[0, layer, i - 1], ag_sem.at[1, layer, i - 1],
                q, 2 * to + c,
            ))

    def gather(layer):
        for i in range(1, N_Z):
            rows = pl.ds(pl.multiple_of(lax.rem(z + N_Z - i, N_Z) * 16, 16), 16)
            view = slot.at[layer, rows]
            remote(view, view, ag_sem.at[0, layer, i - 1], ag_sem.at[1, layer, i - 1], q, other).wait_recv()
        for i, to in enumerate(ahead):
            wides[layer, i] = start(remote(
                slot.at[layer], out_ref.at[layer, c * 16 + q], agxy_sem.at[0, layer, i], agxy_sem.at[1, layer, i], to, b
            ))
        start(remote(
            slot.at[layer], out_ref.at[layer, c * 16 + q], fwd_sem.at[0, layer, 15], fwd_sem.at[1, layer, 15], q, other
        ))
        out_ref[layer, c * 16 + q] = slot[layer]

    def forward(layer):
        for i, came in enumerate(behind):
            view = out_ref.at[layer, c * 16 + came]
            remote(slot.at[layer], view, agxy_sem.at[0, layer, i], agxy_sem.at[1, layer, i], q, other).wait_recv()
            start(remote(view, view, fwd_sem.at[0, layer, i], fwd_sem.at[1, layer, i], q, other))

    def finish(layer):
        for i, came in enumerate(behind + [q]):
            view = out_ref.at[layer, (1 - c) * 16 + came]
            remote(slot.at[layer], view, fwd_sem.at[0, layer, i], fwd_sem.at[1, layer, i], q, other).wait_recv()

    front(0)
    loads["w0"].wait()
    edge_back(0)
    outward(0, 0)
    pl.semaphore_wait(barrier, 1 + (N_Z - 1) + (N_GRP - 1))
    core_send(0, 0)
    outward(0, 1)
    core_send(0, 1)
    chain(0, 0, 0)
    outward(0, 2)
    core_send(0, 2)
    chain(0, 1, 0)
    chain(0, 0, 1)
    loads["x0"].wait()
    weight_grads(0, ITEMS[:9])
    chain(0, 2, 0)
    chain(0, 1, 1)
    chain(0, 0, 2)
    weight_grads(0, ITEMS[9:])
    chain(0, 2, 1)
    chain(0, 1, 2)
    chain(0, 0, 3)
    d_send(0)
    chain(0, 2, 2)
    chain(0, 1, 3)
    chain(0, 0, 4)
    xy_send(0)
    chain(0, 2, 3)
    chain(0, 1, 4)
    chain(0, 2, 4)

    front(1)
    z_send(0)
    loads["x1"].wait()
    weight_grads(1, ITEMS)
    d_send(1)
    z_sum(0)
    loads["w1"].wait()
    edge_back(1)
    xy_send(1)
    outward(1, 0)
    core_send(1, 0)
    outward(1, 1)
    core_send(1, 1)
    gather(0)
    chain(1, 0, 0)
    outward(1, 2)
    core_send(1, 2)
    chain(1, 1, 0)
    chain(1, 0, 1)
    z_send(1)
    chain(1, 2, 0)
    chain(1, 1, 1)
    chain(1, 0, 2)
    z_sum(1)
    chain(1, 2, 1)
    chain(1, 1, 2)
    chain(1, 0, 3)
    gather(1)
    chain(1, 2, 2)
    chain(1, 1, 3)
    chain(1, 0, 4)
    forward(0)
    chain(1, 2, 3)
    chain(1, 1, 4)
    chain(1, 2, 4)
    forward(1)
    finish(0)
    finish(1)
    for copy in started:
        copy.wait_send()


def both_layers(scale, rot, src, tgt, count, top, x_two, x_one, w_two, w_one):
    dma = pltpu.SemaphoreType.DMA
    vmem = pl.BlockSpec(memory_space=pltpu.VMEM)
    hbm = pl.BlockSpec(memory_space=pl.ANY)
    peers = N_GRP - 1
    scratch = [
        pltpu.VMEM((2, COEF, E, C), BF16),
        pltpu.VMEM((2, COEF, C, C), BF16),
        pltpu.VMEM((ROWS, C), F32),
        pltpu.VMEM((AT_ROWS, E), BF16),
        pltpu.VMEM((COEF * C, E), BF16),
        [pltpu.VMEM((width_of(l) * C, height_of(l) * E), BF16) for l in range(7)],
        pltpu.VMEM((N_Z, 2, ROWS, C), F32),
        pltpu.VMEM((2, N_Z, ROWS, C), BF16),
        pltpu.VMEM((2, N_Z, ROWS, C), BF16),
        pltpu.VMEM((2, N_Z - 1, ROWS, C), BF16),
        pltpu.VMEM((2, N_Z - 1, ROWS, C), BF16),
        pltpu.VMEM((2, SLOTS, C, C), F32),
        pltpu.VMEM((2, 16, C, C), F32),
        pltpu.VMEM((2, peers, C, C), BF16),
        pltpu.VMEM((2, peers, C, C), BF16),
        pltpu.VMEM((2, C, C), F32),
        pltpu.VMEM((2, N_Z - 1, 16, C), F32),
        pltpu.VMEM((2, C, C), BF16),
        dma((4,)),
        dma((2, 2, len(CHUNKS))),
        dma((2, 2, len(CHUNKS), N_Z - 1)),
        dma((2, 2)),
        dma((2, 2, peers)),
        dma((2, 2, N_Z - 1)),
        dma((2, 2, N_Z - 1)),
        dma((2, 2, peers)),
        dma((2, 2, N_GRP)),
    ] + [pltpu.VMEM((2 * C, height_of(l) * E), BF16) for l in range(7)]
    return pl.pallas_call(
        functools.partial(kernel, scale),
        out_shape=(
            jax.ShapeDtypeStruct((LIVE, C), F32),
            jax.ShapeDtypeStruct((2, SLOTS, C, C), BF16),
        ),
        in_specs=[vmem] * 5 + [hbm] * 4,
        out_specs=(vmem, vmem),
        scratch_shapes=scratch,
        compiler_params=pltpu.CompilerParams(
            collective_id=0, has_side_effects=True, vmem_limit_bytes=58 * 2**20
        ),
        name="both_layers",
    )(rot, src, tgt, count, top, x_two, x_one, w_two, w_one)


def on_device(
    node_grad, coeffs_one, coeffs_zero, rotations, weight_one, weight_two, sources, targets, edge_count
):
    scale = float(sources.shape[0] * lax.axis_size("grp") * lax.axis_size("bal")) ** (-0.5)
    node, grads = both_layers(
        scale,
        rotations.T,
        sources.reshape(1, E),
        targets.reshape(1, E),
        edge_count.reshape(1, 1),
        jnp.transpose(node_grad, (1, 0, 2)).reshape(LIVE, C),
        jnp.transpose(coeffs_one, (1, 0, 2)),
        jnp.transpose(coeffs_zero, (1, 0, 2)),
        weight_two,
        weight_one,
    )
    node_out = node.reshape(SPHERE, T, C).transpose(1, 0, 2)
    return node_out, grads[1, :COEF].astype(F32), grads[0, :COEF].astype(F32)


def solution(mesh):
    both = P(("grp", "bal"))
    return jax.shard_map(
        on_device,
        mesh=mesh,
        in_specs=(
            P(("grp", "bal"), None, None),
            P(("grp", "bal"), None, None),
            P(("grp", "bal"), None, None),
            P(("grp", "bal"), None),
            P(),
            P(),
            both,
            both,
            both,
        ),
        out_specs=(P(("grp", "bal"), None, None), P(), P()),
        check_vma=False,
    )
```

time: 945 us -> 82 us (0.09); the launches traced: 926 us -> 81.9 us
  waiting for transfers between devices: 597 us -> 0 us
  local copies, waits for them, and re-layouts: 162 us -> 0.68 us
  matrix products: 86.6 us -> 0 us
  Pallas kernels: 0 us -> 76.1 us
  other arithmetic: 64.5 us -> 3.85 us
  between operations: 15.4 us -> 1.3 us
    psum x1 -> x0, waiting for transfers between devices: 373 us -> none  [on_device(): grad_one, grad_two = lax.psum((grad_one, grad_two), ('grp', 'bal'))]
    reduce_scatter x2 -> x0, waiting for transfers between devices: 222 us -> none  [backward_layer(): lax.psum_scatter(node_tile, 'bal', scatter_dimension=0, tiled=True)]
    dot_general x60 -> x0, matrix products: 86.6 us -> none  [the longest x12 40.1 us: rotate_out(): jnp.einsum('emk,emc->ekc', block, picked, precision=lax.Precision.HIGHEST)]
    pallas_call x0 -> x1, Pallas kernels: none -> 76.1 us  [both_layers(): pl.pallas_call(functools.partial(kernel, scale), out_shape=(jax.ShapeDtyp...]
    concatenate x2 -> x0, local copies, waits for them, and re-layouts: 56.6 us -> none  [rotate_out(): return jnp.concatenate(parts, 1)]
    scatter-add x2 -> x0, other arithmetic: 39.7 us -> none  [advance(): return (weight_total + weight_part, node_tile.at[src_block].add(node_back))]
    another operation x9 -> x0, local copies, waits for them, and re-layouts: 34.7 us -> none  [the longest x2 26.9 us: rotate_in(): return jnp.stack(placed, 1)]
    reshape x37 -> x0, local copies, waits for them, and re-layouts: 21.4 us -> none  [the longest x36 20.7 us: rotation_block(): return flat.reshape(flat.shape[0], height, width)]
  transfers between devices with their start and end apart: 3 -> 0, of which waited for: 3 -> 0; matrix products, arithmetic and copies ran while one was open for 0% -> 0% of each run, Pallas kernels for 0% -> 0%
where the time goes in v2:
time: 82 us; the launch traced here: 81.9 us
  Pallas kernels  76.1 us (93%)
  other arithmetic  3.85 us (5%)
  between operations  1.3 us (2%)
    pallas_call x1, Pallas kernels, both_layers(): pl.pallas_call(functools.partial(kernel, scale), out_shape=(jax.ShapeDtyp...  76.1 us
    convert_element_type x1, other arithmetic, on_device(): return (node_out, grads[1, :COEF].astype(F32), grads[0, :COEF].astype(F32))  3.85 us

profile of v2, /device:TPU:1, one launch (start us, length us, event | category | flops | bytes accessed | tf_op | source)
XLA Modules:
  0.0 81.9 jit_solution(9562966959004255743)
XLA Ops:
  1.3 76.1 %both_layers.1 = (f32[392,128]{1,0:T(8,128)}, bf16[2,32,128,128]{3,2,1,0:T(8,128)(2,1)}) custom-call(f32[235,256]{1,0:T(8,128)} %bitcast.21, s32[1,256]{1,0:T(1,128)} %bitcast.24, s32[1,256]{1,0:T(1,128)} %bitcast.25, s32[1,1]{1,0:T(1,128)} %bitcast.18.count_ref, bf16[392,128]{1,0:T(8,128)(2,1)} %bitcast.23, bf16[29,256,128]{2,1,0:T(8,128)(2,1)} %bitcast.19, ...), custom_call_target="tpu_custom_call" | custom-call | tf_op jit(solution)/shard_map/both_layers/pallas_call | solution.py:451
  77.3 0.0 copy-start
  77.4 3.9 %bitcast_convert_fusion = (f32[29,128,128]{2,1,0:T(8,128)}, f32[29,128,128]{2,1,0:T(8,128)}) fusion(bf16[2,32,128,128]{3,2,1,0:T(8,128)(2,1)} %get-tuple-element.6), kind=kLoop, calls=%fused_computation | loop fusion | flops 950272 | bytes 5701632 | tf_op jit(solution)/shard_map/convert_element_type | solution.py:484
  81.2 0.0 copy-done
  81.2 0.7 copy.14
Async XLA Ops:
  77.3 3.9 %copy-start = (f32[392,128]{1,0:T(8,128)S(1)}, f32[392,128]{1,0:T(8,128)}, u32[]{:S(2)}) copy-start(f32[392,128]{1,0:T(8,128)} %get-tuple-element.5) | copy-start | bytes 602116

commit v3 on v2

--- a/solution.py
+++ b/solution.py
@@ -66,7 +66,9 @@
 
 
 SINGLES = tuple(range(7))
-ITEMS = SINGLES + PAIRS
+PARTS = (SINGLES + PAIRS[6:], PAIRS[:6])
+ITEMS = PARTS[0] + PARTS[1]
+PART_SLOTS = ((0, 9), (9, 7))
 CHUNKS = (((6,), 288, 112), ((4, 5), 128, 160), ((0, 1, 2, 3), 0, 128))
 LIVE = SPHERE * T
 OFFSETS = (
@@ -74,6 +76,16 @@
     (2, 0), (0, 2), (2, 1), (1, 2), (2, 3), (3, 2), (2, 2),
 )
 HOP = {("a", 4): 0, ("a", 3): 1, ("a", 2): 2, ("a", 1): 3, ("b", 3): 4, ("b", 2): 5, ("b", 1): 6}
+
+
+def slot_of(r):
+    if 7 <= r <= 18 or r >= 30:
+        j = r - 7 if r <= 18 else r - 18
+        return j // 7, 9 + j % 7
+    a = r if r < 7 else r - 12
+    return a // 9, a % 9
+
+
 STEPS = (
     (("a", 4), ("b", 3)), (("a", 3), ("b", 2)), (("a", 2), ("b", 1)), (("a", 1),), (("own", 0),),
 )
@@ -91,7 +103,7 @@
     rot_ref, src_ref, tgt_ref, count_ref, top_ref, x_two, x_one, w_two, w_one,
     node_ref, out_ref,
     xs, ws, up, at, gt, sbuf, p, cbuf, crecv, hop_s, hop_r,
-    dw, dcore, xy_s, xy_r, zbuf, z_r, slot,
+    dw, dcore, xy_s, xy_r, zbuf, z_r, slot, gath,
     in_sem, c_sem, hop_sem, d_sem, xy_sem, z_sem, ag_sem, agxy_sem, fwd_sem,
     *dxs,
 ):
@@ -163,17 +175,17 @@
         for item in items:
             if isinstance(item, int):
                 g = gt[item * C : (item + 1) * C, :]
-                dw[layer, item] = dot_nn(g, xs[layer, item]).T
+                dw[(layer, *slot_of(item))] = dot_nn(g, xs[layer, item]).T
                 continue
             r, s = item
             g = gt[PLACE[r] * C : (PLACE[r] + 2) * C, :]
             both = dot_nn(g, jnp.concatenate([xs[layer, r], xs[layer, s]], 1))
-            dw[layer, r] = (both[:C, :C] + both[C:, C:]).T
-            dw[layer, s] = (both[C:, :C] - both[:C, C:]).T
+            dw[(layer, *slot_of(r))] = (both[:C, :C] + both[C:, C:]).T
+            dw[(layer, *slot_of(s))] = (both[C:, :C] - both[:C, C:]).T
 
     for layer in range(2):
         for r in range(COEF, SLOTS):
-            dw[layer, r] = jnp.zeros((C, C), F32)
+            dw[(layer, *slot_of(r))] = jnp.zeros((C, C), F32)
 
     def put_dx(r, value):
         high = value.astype(BF16)
@@ -273,24 +285,35 @@
                 hop_s.at[view], hop_r.at[view], hop_sem.at[0, layer, chunk, h], hop_sem.at[1, layer, chunk, h], q, to
             ))
 
-    def d_send(layer):
-        half = pl.ds((1 - c) * 16, 16)
-        cross[layer] = start(remote(
-            dw.at[layer, half], dcore.at[layer], d_sem.at[0, layer], d_sem.at[1, layer], q, other
+    def d_send(layer, part):
+        first, count = PART_SLOTS[part]
+        view = pl.ds(first, count)
+        cross[layer, part] = start(remote(
+            dw.at[layer, 1 - c, view], dcore.at[layer, view], d_sem.at[0, layer, part], d_sem.at[1, layer, part], q, other
         ))
 
-    def xy_send(layer):
-        cross[layer].wait_recv()
-        for i, to in enumerate(ahead):
-            xy_s[layer, i] = (dw[layer, c * 16 + to] + dcore[layer, to]).astype(BF16)
-            planes[layer, i] = start(remote(
-                xy_s.at[layer, i], xy_r.at[layer, i], xy_sem.at[0, layer, i], xy_sem.at[1, layer, i], to, b
-            ))
+    def xy_send(layer, part):
+        cross[layer, part].wait_recv()
+        first, count = PART_SLOTS[part]
+        for i in range(count):
+            to = first + lax.rem(q + i, count)
+
+            @pl.when(to != q)
+            def _():
+                there = lax.rem(to - q + N_GRP, N_GRP) - 1
+                here = lax.rem(q - to + N_GRP, N_GRP) - 1
+                xy_s[layer, there] = (dw[layer, c, to] + dcore[layer, to]).astype(BF16)
+                remote(
+                    xy_s.at[layer, there], xy_r.at[layer, here], xy_sem.at[0, layer], xy_sem.at[1, layer], to, b
+                ).start()
+
+    def plane_all(layer):
+        return remote(xy_s.at[layer], xy_r.at[layer], xy_sem.at[0, layer], xy_sem.at[1, layer], q, other)
 
     def z_send(layer):
-        total = dw[layer, c * 16 + q] + dcore[layer, q]
+        plane_all(layer).wait_recv()
+        total = dw[layer, c, q] + dcore[layer, q]
         for i in range(N_GRP - 1):
-            planes[layer, i].wait_recv()
             total += xy_r[layer, i].astype(F32)
         zbuf[layer] = total
         for i in range(1, N_Z):
@@ -323,23 +346,30 @@
             remote(view, view, ag_sem.at[0, layer, i - 1], ag_sem.at[1, layer, i - 1], q, other).wait_recv()
         for i, to in enumerate(ahead):
             wides[layer, i] = start(remote(
-                slot.at[layer], out_ref.at[layer, c * 16 + q], agxy_sem.at[0, layer, i], agxy_sem.at[1, layer, i], to, b
+                slot.at[layer], gath.at[layer, c, q], agxy_sem.at[0, layer, i], agxy_sem.at[1, layer, i], to, b
             ))
-        start(remote(
-            slot.at[layer], out_ref.at[layer, c * 16 + q], fwd_sem.at[0, layer, 15], fwd_sem.at[1, layer, 15], q, other
-        ))
-        out_ref[layer, c * 16 + q] = slot[layer]
+        gath[layer, c, q] = slot[layer]
 
     def forward(layer):
-        for i, came in enumerate(behind):
-            view = out_ref.at[layer, c * 16 + came]
-            remote(slot.at[layer], view, agxy_sem.at[0, layer, i], agxy_sem.at[1, layer, i], q, other).wait_recv()
-            start(remote(view, view, fwd_sem.at[0, layer, i], fwd_sem.at[1, layer, i], q, other))
+        for dx in range(4):
+            for i, came in enumerate(behind):
+                if OFFSETS[i][0] == dx:
+                    remote(
+                        slot.at[layer], gath.at[layer, c, came], agxy_sem.at[0, layer, i], agxy_sem.at[1, layer, i], q, other
+                    ).wait_recv()
+            view = gath.at[layer, c, pl.ds(plane(4 - dx, 0) - py, 4)]
+            start(remote(view, view, fwd_sem.at[0, layer, dx], fwd_sem.at[1, layer, dx], q, other))
 
     def finish(layer):
-        for i, came in enumerate(behind + [q]):
-            view = out_ref.at[layer, (1 - c) * 16 + came]
-            remote(slot.at[layer], view, fwd_sem.at[0, layer, i], fwd_sem.at[1, layer, i], q, other).wait_recv()
+        for dx in range(4):
+            view = gath.at[layer, 1 - c, pl.ds(plane(4 - dx, 0) - py, 4)]
+            remote(view, view, fwd_sem.at[0, layer, dx], fwd_sem.at[1, layer, dx], q, other).wait_recv()
+        for r in range(COEF):
+            out_ref[layer, r] = gath[(layer, *slot_of(r))]
+
+    def chains(layer, step):
+        for chunk in range(len(CHUNKS)):
+            chain(layer, chunk, step)
 
     front(0)
     loads["w0"].wait()
@@ -353,71 +383,68 @@
     outward(0, 2)
     core_send(0, 2)
     chain(0, 1, 0)
-    chain(0, 0, 1)
     loads["x0"].wait()
-    weight_grads(0, ITEMS[:9])
+    weight_grads(0, ITEMS[:4])
     chain(0, 2, 0)
-    chain(0, 1, 1)
-    chain(0, 0, 2)
-    weight_grads(0, ITEMS[9:])
-    chain(0, 2, 1)
-    chain(0, 1, 2)
-    chain(0, 0, 3)
-    d_send(0)
-    chain(0, 2, 2)
-    chain(0, 1, 3)
-    chain(0, 0, 4)
-    xy_send(0)
-    chain(0, 2, 3)
-    chain(0, 1, 4)
-    chain(0, 2, 4)
+    weight_grads(0, ITEMS[4:8])
+    chains(0, 1)
+    weight_grads(0, ITEMS[8:12])
+    d_send(0, 0)
+    chains(0, 2)
+    weight_grads(0, ITEMS[12:])
+    d_send(0, 1)
+    chains(0, 3)
+    chains(0, 4)
 
     front(1)
-    z_send(0)
+    xy_send(0, 0)
+    xy_send(0, 1)
     loads["x1"].wait()
-    weight_grads(1, ITEMS)
-    d_send(1)
-    z_sum(0)
+    weight_grads(1, PARTS[0])
+    d_send(1, 0)
+    weight_grads(1, PARTS[1])
+    d_send(1, 1)
     loads["w1"].wait()
     edge_back(1)
-    xy_send(1)
+    xy_send(1, 0)
     outward(1, 0)
     core_send(1, 0)
+    xy_send(1, 1)
     outward(1, 1)
     core_send(1, 1)
-    gather(0)
+    z_send(0)
     chain(1, 0, 0)
     outward(1, 2)
     core_send(1, 2)
     chain(1, 1, 0)
-    chain(1, 0, 1)
+    chain(1, 2, 0)
+    z_sum(0)
+    chains(1, 1)
     z_send(1)
-    chain(1, 2, 0)
-    chain(1, 1, 1)
-    chain(1, 0, 2)
+    gather(0)
+    chains(1, 2)
     z_sum(1)
-    chain(1, 2, 1)
-    chain(1, 1, 2)
-    chain(1, 0, 3)
+    chains(1, 3)
     gather(1)
-    chain(1, 2, 2)
-    chain(1, 1, 3)
-    chain(1, 0, 4)
+    chains(1, 4)
     forward(0)
-    chain(1, 2, 3)
-    chain(1, 1, 4)
-    chain(1, 2, 4)
+    late = started[-4:] + list(wides.values())
+    early = [copy for copy in started if not any(copy is other_copy for other_copy in late)]
+    plane_all(0).wait_send()
+    plane_all(1).wait_send()
+    for copy in early:
+        copy.wait_send()
+    finish(0)
     forward(1)
-    finish(0)
+    for copy in late + started[-4:]:
+        copy.wait_send()
     finish(1)
-    for copy in started:
-        copy.wait_send()
 
 
 def both_layers(scale, rot, src, tgt, count, top, x_two, x_one, w_two, w_one):
     dma = pltpu.SemaphoreType.DMA
     vmem = pl.BlockSpec(memory_space=pltpu.VMEM)
-    hbm = pl.BlockSpec(memory_space=pl.ANY)
+    hbm = pl.BlockSpec(memory_space=pltpu.HBM)
     peers = N_GRP - 1
     scratch = [
         pltpu.VMEM((2, COEF, E, C), BF16),
@@ -431,28 +458,29 @@
         pltpu.VMEM((2, N_Z, ROWS, C), BF16),
         pltpu.VMEM((2, N_Z - 1, ROWS, C), BF16),
         pltpu.VMEM((2, N_Z - 1, ROWS, C), BF16),
-        pltpu.VMEM((2, SLOTS, C, C), F32),
-        pltpu.VMEM((2, 16, C, C), F32),
+        pltpu.VMEM((2, 2, N_GRP, C, C), F32),
+        pltpu.VMEM((2, N_GRP, C, C), F32),
         pltpu.VMEM((2, peers, C, C), BF16),
         pltpu.VMEM((2, peers, C, C), BF16),
         pltpu.VMEM((2, C, C), F32),
         pltpu.VMEM((2, N_Z - 1, 16, C), F32),
         pltpu.VMEM((2, C, C), BF16),
+        pltpu.VMEM((2, 2, N_GRP, C, C), BF16),
         dma((4,)),
         dma((2, 2, len(CHUNKS))),
         dma((2, 2, len(CHUNKS), N_Z - 1)),
+        dma((2, 2, 2)),
         dma((2, 2)),
-        dma((2, 2, peers)),
         dma((2, 2, N_Z - 1)),
         dma((2, 2, N_Z - 1)),
         dma((2, 2, peers)),
-        dma((2, 2, N_GRP)),
+        dma((2, 2, 4)),
     ] + [pltpu.VMEM((2 * C, height_of(l) * E), BF16) for l in range(7)]
     return pl.pallas_call(
         functools.partial(kernel, scale),
         out_shape=(
             jax.ShapeDtypeStruct((LIVE, C), F32),
-            jax.ShapeDtypeStruct((2, SLOTS, C, C), BF16),
+            pltpu.VMEM((2, COEF, C, C), BF16),
         ),
         in_specs=[vmem] * 5 + [hbm] * 4,
         out_specs=(vmem, vmem),
@@ -481,7 +509,7 @@
         weight_one,
     )
     node_out = node.reshape(SPHERE, T, C).transpose(1, 0, 2)
-    return node_out, grads[1, :COEF].astype(F32), grads[0, :COEF].astype(F32)
+    return node_out, grads[1].astype(F32), grads[0].astype(F32)
 
 
 def solution(mesh):

time: 82 us -> 73.5 us (0.90)
  Pallas kernels: 76.1 us -> 69.1 us
  other arithmetic: 3.85 us -> 2.34 us
    pallas_call x1, Pallas kernels: 76.1 us -> 69.1 us  [both_layers(): pl.pallas_call(functools.partial(kernel, scale), out_shape=(jax.ShapeDtyp...]
    convert_element_type x1, other arithmetic: 3.85 us -> 2.34 us  [on_device(): return (node_out, grads[1].astype(F32), grads[0].astype(F32))]
where the time goes in v3:
time: 73.5 us; the launch traced here: 73.4 us
  Pallas kernels  69.1 us (94%)
  other arithmetic  2.34 us (3%)
  between operations  1.3 us (2%)
    pallas_call x1, Pallas kernels, both_layers(): pl.pallas_call(functools.partial(kernel, scale), out_shape=(jax.ShapeDtyp...  69.1 us
    convert_element_type x1, other arithmetic, on_device(): return (node_out, grads[1].astype(F32), grads[0].astype(F32))  2.34 us

profile of v3, /device:TPU:1, one launch (start us, length us, event | category | flops | bytes accessed | tf_op | source)
XLA Modules:
  0.0 73.4 jit_solution(15187813722044474750)
XLA Ops:
  1.3 69.1 %both_layers.1 = (f32[392,128]{1,0:T(8,128)}, bf16[2,29,128,128]{3,2,1,0:T(8,128)(2,1)S(1)}) custom-call(f32[235,256]{1,0:T(8,128)} %bitcast.21, s32[1,256]{1,0:T(1,128)} %bitcast.24, s32[1,256]{1,0:T(1,128)} %bitcast.25, s32[1,1]{1,0:T(1,128)} %bitcast.18.count_ref, bf16[392,128]{1,0:T(8,128)(2,1)} %bitcast.23, bf16[29,256,128]{2,1,0:T(8,128)(2,1)} %bitcast.19, ...), custom_call_target="tpu_custom_call" | custom-call | tf_op jit(solution)/shard_map/both_layers/pallas_call | solution.py:479
  70.4 0.0 copy-start
  70.4 2.3 %bitcast_convert_fusion = (f32[29,128,128]{2,1,0:T(8,128)}, f32[29,128,128]{2,1,0:T(8,128)}) fusion(bf16[2,29,128,128]{3,2,1,0:T(8,128)(2,1)S(1)} %get-tuple-element.6), kind=kLoop, calls=%fused_computation | loop fusion | flops 950272 | bytes 5701632 | tf_op jit(solution)/shard_map/convert_element_type | solution.py:512
  72.7 0.0 copy-done
  72.7 0.7 copy.14
Async XLA Ops:
  70.4 2.4 %copy-start = (f32[392,128]{1,0:T(8,128)S(1)}, f32[392,128]{1,0:T(8,128)}, u32[]{:S(2)}) copy-start(f32[392,128]{1,0:T(8,128)} %get-tuple-element.5) | copy-start | bytes 602116

commit v4 on v3

--- a/solution.py
+++ b/solution.py
@@ -68,12 +68,13 @@
 SINGLES = tuple(range(7))
 PARTS = (SINGLES + PAIRS[6:], PAIRS[:6])
 ITEMS = PARTS[0] + PARTS[1]
+OF_DEGREE = tuple((l,) + ((PAIRS[l - 1],) if l > 0 else ()) + ((PAIRS[l + 4],) if l > 1 else ()) for l in range(7))
 PART_SLOTS = ((0, 9), (9, 7))
 CHUNKS = (((6,), 288, 112), ((4, 5), 128, 160), ((0, 1, 2, 3), 0, 128))
 LIVE = SPHERE * T
 OFFSETS = (
-    (1, 0), (0, 1), (3, 0), (0, 3), (1, 1), (3, 3), (1, 3), (3, 1),
-    (2, 0), (0, 2), (2, 1), (1, 2), (2, 3), (3, 2), (2, 2),
+    (2, 2), (2, 1), (1, 2), (2, 3), (3, 2), (2, 0), (0, 2), (1, 1),
+    (3, 3), (1, 3), (3, 1), (1, 0), (0, 1), (3, 0), (0, 3),
 )
 HOP = {("a", 4): 0, ("a", 3): 1, ("a", 2): 2, ("a", 1): 3, ("b", 3): 4, ("b", 2): 5, ("b", 1): 6}
 
@@ -143,13 +144,13 @@
     up[LIVE:ROWS] = jnp.zeros((ROWS - LIVE, C), F32)
     p[:, :, LIVE:ROWS] = jnp.zeros((N_Z, 2, ROWS - LIVE, C), F32)
 
-    def front(layer):
+    def front(layer, degrees):
         if layer == 0:
             lane = lax.broadcasted_iota(jnp.int32, (T, E), 1)
             spot = lax.broadcasted_iota(jnp.int32, (T, E), 0)
             hit = (spot == tgt_ref[...] - b * T) & (lane < count_ref[...])
             hot = jnp.where(hit, 1.0, 0.0).astype(F32)
-        for l in range(7):
+        for l in degrees:
             width, height, depth = width_of(l), height_of(l), depth_of(l)
             rest = depth - 2 * T * width
             rows = up[T * l * l : T * (l + 1) * (l + 1), :]
@@ -175,13 +176,13 @@
         for item in items:
             if isinstance(item, int):
                 g = gt[item * C : (item + 1) * C, :]
-                dw[(layer, *slot_of(item))] = dot_nn(g, xs[layer, item]).T
+                dw[(layer, *slot_of(item))] = dot_nn(g, xs[layer, item])
                 continue
             r, s = item
             g = gt[PLACE[r] * C : (PLACE[r] + 2) * C, :]
             both = dot_nn(g, jnp.concatenate([xs[layer, r], xs[layer, s]], 1))
-            dw[(layer, *slot_of(r))] = (both[:C, :C] + both[C:, C:]).T
-            dw[(layer, *slot_of(s))] = (both[C:, :C] - both[:C, C:]).T
+            dw[(layer, *slot_of(r))] = both[:C, :C] + both[C:, C:]
+            dw[(layer, *slot_of(s))] = both[C:, :C] - both[:C, C:]
 
     for layer in range(2):
         for r in range(COEF, SLOTS):
@@ -196,8 +197,8 @@
                     dxs[l][0:C, m * E : (m + 1) * E] = high
                     dxs[l][C : 2 * C, m * E : (m + 1) * E] = low
 
-    def edge_back(layer):
-        for item in ITEMS:
+    def edge_back(layer, degrees):
+        for item in [i for l in degrees for i in OF_DEGREE[l]]:
             if isinstance(item, int):
                 put_dx(item, dot_nn(ws[layer, item], gt[item * C : (item + 1) * C, :]))
                 continue
@@ -315,7 +316,7 @@
         total = dw[layer, c, q] + dcore[layer, q]
         for i in range(N_GRP - 1):
             total += xy_r[layer, i].astype(F32)
-        zbuf[layer] = total
+        zbuf[layer] = total.T
         for i in range(1, N_Z):
             to = lax.rem(z + i, N_Z)
             rows = pl.ds(pl.multiple_of(to * 16, 16), 16)
@@ -371,50 +372,56 @@
         for chunk in range(len(CHUNKS)):
             chain(layer, chunk, step)
 
-    front(0)
+    def back_chunk(layer, chunk):
+        edge_back(layer, CHUNKS[chunk][0])
+        outward(layer, chunk)
+
+    front(0, CHUNKS[0][0])
     loads["w0"].wait()
-    edge_back(0)
-    outward(0, 0)
+    back_chunk(0, 0)
     pl.semaphore_wait(barrier, 1 + (N_Z - 1) + (N_GRP - 1))
     core_send(0, 0)
-    outward(0, 1)
+    front(0, CHUNKS[1][0])
+    back_chunk(0, 1)
     core_send(0, 1)
     chain(0, 0, 0)
-    outward(0, 2)
+    front(0, CHUNKS[2][0])
+    back_chunk(0, 2)
     core_send(0, 2)
     chain(0, 1, 0)
     loads["x0"].wait()
-    weight_grads(0, ITEMS[:4])
+    weight_grads(0, PARTS[0])
+    d_send(0, 0)
     chain(0, 2, 0)
-    weight_grads(0, ITEMS[4:8])
     chains(0, 1)
-    weight_grads(0, ITEMS[8:12])
-    d_send(0, 0)
+    weight_grads(0, PARTS[1])
+    d_send(0, 1)
     chains(0, 2)
-    weight_grads(0, ITEMS[12:])
-    d_send(0, 1)
-    chains(0, 3)
-    chains(0, 4)
-
-    front(1)
     xy_send(0, 0)
     xy_send(0, 1)
+    chains(0, 3)
+    chain(0, 0, 4)
+    front(1, CHUNKS[0][0])
+    chain(0, 1, 4)
+
+    front(1, CHUNKS[1][0])
+    chain(0, 2, 4)
+    front(1, CHUNKS[2][0])
     loads["x1"].wait()
     weight_grads(1, PARTS[0])
     d_send(1, 0)
     weight_grads(1, PARTS[1])
     d_send(1, 1)
+    z_send(0)
     loads["w1"].wait()
-    edge_back(1)
+    back_chunk(1, 0)
+    core_send(1, 0)
     xy_send(1, 0)
-    outward(1, 0)
-    core_send(1, 0)
+    back_chunk(1, 1)
+    core_send(1, 1)
     xy_send(1, 1)
-    outward(1, 1)
-    core_send(1, 1)
-    z_send(0)
     chain(1, 0, 0)
-    outward(1, 2)
+    back_chunk(1, 2)
     core_send(1, 2)
     chain(1, 1, 0)
     chain(1, 2, 0)

time: 73.5 us -> 72.3 us (0.984)
  Pallas kernels: 69.1 us -> 67.8 us
    pallas_call x1, Pallas kernels: 69.1 us -> 67.8 us  [both_layers(): pl.pallas_call(functools.partial(kernel, scale), out_shape=(jax.ShapeDtyp...]
where the time goes in v4:
time: 72.3 us; the launch traced here: 72.1 us
  Pallas kernels  67.8 us (94%)
  other arithmetic  2.34 us (3%)
  between operations  1.3 us (2%)
    pallas_call x1, Pallas kernels, both_layers(): pl.pallas_call(functools.partial(kernel, scale), out_shape=(jax.ShapeDtyp...  67.8 us
    convert_element_type x1, other arithmetic, on_device(): return (node_out, grads[1].astype(F32), grads[0].astype(F32))  2.34 us

profile of v4, /device:TPU:1, one launch (start us, length us, event | category | flops | bytes accessed | tf_op | source)
XLA Modules:
  0.0 72.1 jit_solution(10820965061293171499)
XLA Ops:
  1.3 67.8 %both_layers.1 = (f32[392,128]{1,0:T(8,128)}, bf16[2,29,128,128]{3,2,1,0:T(8,128)(2,1)S(1)}) custom-call(f32[235,256]{1,0:T(8,128)} %bitcast.21, s32[1,256]{1,0:T(1,128)} %bitcast.24, s32[1,256]{1,0:T(1,128)} %bitcast.25, s32[1,1]{1,0:T(1,128)} %bitcast.18.count_ref, bf16[392,128]{1,0:T(8,128)(2,1)} %bitcast.23, bf16[29,256,128]{2,1,0:T(8,128)(2,1)} %bitcast.19, ...), custom_call_target="tpu_custom_call" | custom-call | tf_op jit(solution)/shard_map/both_layers/pallas_call | solution.py:486
  69.1 0.0 copy-start
  69.1 2.3 %bitcast_convert_fusion = (f32[29,128,128]{2,1,0:T(8,128)}, f32[29,128,128]{2,1,0:T(8,128)}) fusion(bf16[2,29,128,128]{3,2,1,0:T(8,128)(2,1)S(1)} %get-tuple-element.6), kind=kLoop, calls=%fused_computation | loop fusion | flops 950272 | bytes 5701632 | tf_op jit(solution)/shard_map/convert_element_type | solution.py:519
  71.5 0.0 copy-done
  71.5 0.7 copy.14
Async XLA Ops:
  69.1 2.4 %copy-start = (f32[392,128]{1,0:T(8,128)S(1)}, f32[392,128]{1,0:T(8,128)}, u32[]{:S(2)}) copy-start(f32[392,128]{1,0:T(8,128)} %get-tuple-element.5) | copy-start | bytes 602116
